TPU v7x, 32 devices: a whole 2x2x4 slice. The times are simulated.
32 devices in a mesh: row: 4 (over y, x), col: 8 (over z, core).
Axes of the slice: x: 2, y: 2, z: 4, core: 2. Of those that a mesh axis runs over, the one named last changes fastest.
Arguments:
- gram: float32 [4096, 4096], P('row', 'col'), may hold values from -6 to 8
- rotations: float32 [2, 4, 1024, 1024], P(None, 'row', 'col'), may hold values from -1 to 2
Outputs:
- rotated: float32 [4096, 4096], P('row', 'col')
All inputs are finite; a program needn't handle non-finite values.
Results may differ from a plain program's by a relative error of at most 0.00016.
Values sent between devices are 32-bit elements; how exact they have to be, the bound alone decides.
A program may use at most 64 MiB of HBM per device.

v0:
```python
import jax
import jax.numpy as jnp
from jax import lax
from jax.sharding import PartitionSpec as P


def broadcast(block, axis, source):
    block = jnp.where(lax.axis_index(axis) == source, block, jnp.zeros_like(block))
    return lax.psum(block, axis)


def from_partner(value, axis, stride):
    mask = 2**stride
    pairs = [(source, source ^ mask) for source in range(lax.axis_size(axis))]
    return lax.ppermute(value, axis, pairs)


def passed_along(value, axis, steps):
    count = lax.axis_size(axis)
    first, last = (max(0, -steps), min(count, count - steps))
    return lax.ppermute(value, axis, [(source, source + steps) for source in range(first, last)])


def mix_rows(turn, mixed):
    return lax.dot_general(
        turn,
        mixed,
        (((0,), (0,)), ((), ())),
        precision=lax.Precision.HIGHEST,
        preferred_element_type=jnp.float32,
    )


def shards(gram, rotations):
    n_row = lax.axis_size("row")
    n_col = lax.axis_size("col")
    row_index = lax.axis_index("row")
    col_index = lax.axis_index("col")
    width = gram.shape[1]
    steps_count = rotations.shape[0]
    parity = col_index % 2
    root = col_index // 2
    last_pair = n_col // 2 - 1
    whole_all = lax.all_gather(rotations[:, 0], "col", axis=1, tiled=True)
    halves = lax.dynamic_slice_in_dim(whole_all, parity * width, width, 2)
    column_all = broadcast(halves, "row", root)
    current = gram
    for step in range(steps_count):
        whole = whole_all[step]
        column_turn = column_all[step]
        partner = from_partner(current, "col", 0)
        first = jnp.where(parity == 0, current, partner)
        second = jnp.where(parity == 0, partner, current)
        mixed = jnp.dot(
            first,
            column_turn[:width],
            precision=lax.Precision.HIGHEST,
            preferred_element_type=jnp.float32,
        )
        mixed = mixed + jnp.dot(
            second,
            column_turn[width:],
            precision=lax.Precision.HIGHEST,
            preferred_element_type=jnp.float32,
        )
        turned = mix_rows(whole, mixed)
        top_own = turned[:width]
        bottom_own = turned[width:]
        give = jnp.where(parity == 0, bottom_own, top_own)
        taken = from_partner(give, "col", 0)
        mine = jnp.where(parity == 0, top_own, bottom_own)
        even_half = jnp.where(parity == 0, mine, taken)
        odd_half = jnp.where(parity == 0, taken, mine)
        upward = jnp.where(root == 0, odd_half, even_half)
        from_left = passed_along(upward, "col", 2)
        from_right = passed_along(odd_half, "col", -2)
        first_half = jnp.where(root == 0, even_half, from_left)
        second_half = jnp.where(root == last_pair, even_half, from_right)
        handed = jnp.where(parity == 0, second_half, first_half)
        joined = from_partner(handed, "col", 0)
        moved = jnp.where(
            parity == 0,
            jnp.concatenate([first_half, joined], axis=0),
            jnp.concatenate([joined, second_half], axis=0),
        )
        upper = moved[:width]
        lower = moved[width:]
        send_up = jnp.where(row_index == 0, lower, upper)
        arrived_up = passed_along(send_up, "row", 1)
        arrived_down = passed_along(lower, "row", -1)
        new_upper = jnp.where(row_index == 0, upper, arrived_up)
        new_lower = jnp.where(row_index == n_row - 1, upper, arrived_down)
        current = jnp.concatenate([new_upper, new_lower], axis=0)
    return current


def solution(mesh):
    placed = (P("row", "col"), P(None, "row", "col", None))
    return jax.shard_map(
        shards, mesh=mesh, in_specs=placed, out_specs=P("row", "col"), check_vma=False
    )
```

profile of v0, /device:TPU:26, one launch (start us, length us, event | category | flops | bytes accessed | tf_op | source)
XLA Modules:
  0.0 430.0 jit_solution(8312216617847759300)
XLA Ops:
  7.3 82.2 %all-gather.3.cloned.1.call-done = f32[2,1,1024,1024]{3,2,1,0:T(8,128)} async-done(((f32[2,1,128,1024]{3,2,1,0:T(8,128)}), f32[2,1,1024,1024]{3,2,1,0:T(8,128)}) %all-gather.3.cloned.1.call-update) | async-done | bytes 8388624 | tf_op jit(solution)/shard_map/all_gather | solution.py:44
  89.5 4.6 %select_bitcast_fusion = f32[2,1024,512]{2,1,0:T(8,128)} fusion(f32[2,1,1024,1024]{3,2,1,0:T(8,128)} %all-gather.3.cloned.1.call-done, s32[]{:T(128)S(6)} %select_n.158, pred[]{:T(512)S(6)} %eq.17), kind=kLoop, calls=%fused_computation.4 | loop fusion | flops 1048576 | bytes 8388613 | tf_op jit(solution)/shard_map/jit(_where)/select_n | solution.py:8
  94.2 1.9 copy.4
  96.4 4.0 collective-permute-done
  100.5 98.7 %all-reduce.2.cloned.1.call-done = f32[2,1024,512]{2,1,0:T(8,128)} async-done(((f32[2,1024,512]{2,1,0:T(8,128)}), f32[2,1024,512]{2,1,0:T(8,128)}) %all-reduce.2.cloned.1.call-update) | async-done | bytes 4194320 | tf_op jit(solution)/shard_map/psum | solution.py:9
  199.2 5.4 %fusion.8 = f32[1024,512]{1,0:T(8,128)S(1)} fusion(f32[1024,512]{0,1:T(8,128)} %collective-permute-done, f32[1024,512]{0,1:T(8,128)S(1)} %copy.4, f32[2,1024,512]{2,1,0:T(8,128)} %all-reduce.2.cloned.1.call-done, pred[]{:T(512)S(6)} %eq.15), kind=kOutput, calls=%fused_computation.15 | convolution fusion | flops 3221749760 | bytes 7340033 | tf_op jit(solution)/shard_map/dot_general | solution.py:60
  204.6 4.8 %fusion.10 = f32[1024,512]{1,0:T(8,128)S(1)} fusion(f32[1024,512]{0,1:T(8,128)S(1)} %copy.4, f32[1024,512]{0,1:T(8,128)} %collective-permute-done, f32[2,1024,512]{2,1,0:T(8,128)} %all-reduce.2.cloned.1.call-done, pred[]{:T(512)S(6)} %eq.15), kind=kOutput, calls=%fused_computation.17 | convolution fusion | flops 3221749760 | bytes 7340033 | tf_op jit(solution)/shard_map/dot_general | solution.py:54
  209.4 9.2 %fusion.12 = f32[1024,512]{0,1:T(8,128)S(1)} fusion(f32[2,1,1024,1024]{3,2,1,0:T(8,128)} %all-gather.3.cloned.1.call-done, f32[1024,512]{1,0:T(8,128)S(1)} %fusion.10, f32[1024,512]{1,0:T(8,128)S(1)} %fusion.8), kind=kOutput, calls=%fused_computation.19 | convolution fusion | flops 6442975232 | bytes 10485760 | tf_op jit(solution)/shard_map/dot_general | solution.py:25
  218.9 2.8 collective-permute-done.1
  221.7 3.0 broadcast_select_fusion.11
  226.0 4.6 %collective-permute-start.3 = (f32[512,512]{0,1:T(8,128)}, f32[512,512]{0,1:T(8,128)S(1)}, u32[]{:S(2)}, u32[]{:S(2)}) collective-permute-start(f32[512,512]{0,1:T(8,128)} %get-tuple-element.15), channel_id=1, source_target_pairs={{2,0},{3,1},{4,2},{5,3},{6,4},{7,5},{10,8},{11,9},{12,10},{13,11},... | collective-permute-start | bytes 3145736 | tf_op jit(solution)/shard_map/ppermute | solution.py:21
  230.6 21.4 %collective-permute-done.2 = f32[512,512]{0,1:T(8,128)S(1)} collective-permute-done((f32[512,512]{0,1:T(8,128)}, f32[512,512]{0,1:T(8,128)S(1)}, u32[]{:S(2)}, u32[]{:S(2)}) %collective-permute-start.2) | collective-permute-done | bytes 1048608 | tf_op jit(solution)/shard_map/ppermute | solution.py:21
  256.0 2.9 collective-permute-done.4
  259.8 2.2 maximum_select_fusion
  263.3 3.2 collective-permute-start.5
  266.5 3.6 collective-permute-start.6
  270.1 20.6 %collective-permute-done.5 = f32[512,512]{0,1:T(8,128)} collective-permute-done((f32[512,512]{0,1:T(8,128)}, f32[512,512]{0,1:T(8,128)}, u32[]{:S(2)}, u32[]{:S(2)}) %collective-permute-start.5) | collective-permute-done | bytes 1048608 | tf_op jit(solution)/shard_map/ppermute | solution.py:21
  290.7 22.5 %collective-permute-done.6 = f32[512,512]{0,1:T(8,128)} collective-permute-done((f32[512,512]{0,1:T(8,128)S(1)}, f32[512,512]{0,1:T(8,128)}, u32[]{:S(2)}, u32[]{:S(2)}) %collective-permute-start.6) | collective-permute-done | bytes 1048608 | tf_op jit(solution)/shard_map/ppermute | solution.py:21
  313.1 2.1 slice_select_fusion.8
  315.5 4.1 collective-permute-done.7
  319.6 3.6 fusion.3
  323.2 3.6 fusion.5
  326.8 7.2 %fusion.15 = f32[1024,512]{0,1:T(8,128)S(1)} fusion(f32[2,1,1024,1024]{3,2,1,0:T(8,128)S(1)} %bitcast.29, f32[1024,512]{1,0:T(8,128)S(1)} %fusion.5, f32[1024,512]{1,0:T(8,128)S(1)} %fusion.3), kind=kOutput, calls=%fused_computation.20 | convolution fusion | flops 6442975232 | bytes 10485760 | tf_op jit(solution)/shard_map/dot_general | solution.py:25
  334.4 2.5 collective-permute-done.8
  337.4 5.6 %collective-permute-start.10 = (f32[512,512]{0,1:T(8,128)S(1)}, f32[512,512]{0,1:T(8,128)S(1)}, u32[]{:S(2)}, u32[]{:S(2)}) collective-permute-start(f32[512,512]{0,1:T(8,128)S(1)} %get-tuple-element.9), channel_id=1, source_target_pairs={{2,0},{3,1},{4,2},{5,3},{6,4},{7,5},{10,8},{11,9},{12,10},{13,11},... | collective-permute-start | bytes 3145736 | tf_op jit(solution)/shard_map/ppermute | solution.py:21
  344.3 21.3 %collective-permute-done.10 = f32[512,512]{0,1:T(8,128)S(1)} collective-permute-done((f32[512,512]{0,1:T(8,128)S(1)}, f32[512,512]{0,1:T(8,128)S(1)}, u32[]{:S(2)}, u32[]{:S(2)}) %collective-permute-start.10) | collective-permute-done | bytes 1048608 | tf_op jit(solution)/shard_map/ppermute | solution.py:21
  365.6 4.2 collective-permute-done.9
  370.2 2.6 collective-permute-done.11
  373.5 1.9 collective-permute-start.12
  375.4 4.0 collective-permute-start.13
  379.4 21.2 %collective-permute-done.12 = f32[512,512]{0,1:T(8,128)S(1)} collective-permute-done((f32[512,512]{0,1:T(8,128)S(1)}, f32[512,512]{0,1:T(8,128)S(1)}, u32[]{:S(2)}, u32[]{:S(2)}) %collective-permute-start.12) | collective-permute-done | bytes 1048608 | tf_op jit(solution)/shard_map/ppermute | solution.py:21
  400.6 20.3 %collective-permute-done.13 = f32[512,512]{0,1:T(8,128)S(1)} collective-permute-done((f32[512,512]{0,1:T(8,128)S(1)}, f32[512,512]{0,1:T(8,128)S(1)}, u32[]{:S(2)}, u32[]{:S(2)}) %collective-permute-start.13) | collective-permute-done | bytes 1048608 | tf_op jit(solution)/shard_map/ppermute | solution.py:21
  (36 shorter events, 14.6 us)
Async XLA Ops:
  6.5 83.0 %all-gather.3.cloned.1.call-start = ((), (), s32[]{:S(2)}) async-start(), calls=%async_computation.1 | async-start | bytes 9437184 | tf_op jit(solution)/shard_map/all_gather | solution.py:44
  7.3 191.9 %all-reduce.2.cloned.1.call-start = ((), (), s32[]{:S(2)}) async-start(), calls=%async_computation | async-start | bytes 8388608 | tf_op jit(solution)/shard_map/psum | solution.py:9
  96.1 4.4 %collective-permute-start = (f32[1024,512]{0,1:T(8,128)S(1)}, f32[1024,512]{0,1:T(8,128)}, u32[]{:S(2)}, u32[]{:S(2)}) collective-permute-start(f32[1024,512]{0,1:T(8,128)S(1)} %copy.4), channel_id=1, source_target_pairs={{0,1},{1,0},{2,3},{3,2},{4,5},{5,4},{6,7},{7,6},{8,9},{9,8},{10,11... | collective-permute-start | bytes 6291464 | tf_op jit(solution)/shard_map/ppermute | solution.py:15
  218.8 2.9 collective-permute-start.1
  224.7 27.3 %collective-permute-start.2 = (f32[512,512]{0,1:T(8,128)}, f32[512,512]{0,1:T(8,128)S(1)}, u32[]{:S(2)}, u32[]{:S(2)}) collective-permute-start(f32[512,512]{0,1:T(8,128)} %get-tuple-element.14), channel_id=1, source_target_pairs={{0,2},{1,3},{2,4},{3,5},{4,6},{5,7},{8,10},{9,11},{10,12},{11,13},... | collective-permute-start | bytes 3145736 | tf_op jit(solution)/shard_map/ppermute | solution.py:21
  226.0 27.3 %collective-permute-start.3 = (f32[512,512]{0,1:T(8,128)}, f32[512,512]{0,1:T(8,128)S(1)}, u32[]{:S(2)}, u32[]{:S(2)}) collective-permute-start(f32[512,512]{0,1:T(8,128)} %get-tuple-element.15), channel_id=1, source_target_pairs={{2,0},{3,1},{4,2},{5,3},{6,4},{7,5},{10,8},{11,9},{12,10},{13,11},... | collective-permute-start | bytes 3145736 | tf_op jit(solution)/shard_map/ppermute | solution.py:21
  253.3 1.0 copy-start.1
  256.0 2.9 collective-permute-start.4
  258.8 1.0 copy-start.2
  263.3 27.4 %collective-permute-start.5 = (f32[512,512]{0,1:T(8,128)}, f32[512,512]{0,1:T(8,128)}, u32[]{:S(2)}, u32[]{:S(2)}) collective-permute-start(f32[512,512]{0,1:T(8,128)} %get-tuple-element.23), channel_id=1, source_target_pairs={{0,8},{8,16},{16,24},{1,9},{9,17},{17,25},{2,10},{10,18},{18,26},{... | collective-permute-start | bytes 3145736 | tf_op jit(solution)/shard_map/ppermute | solution.py:21
  266.5 46.6 %collective-permute-start.6 = (f32[512,512]{0,1:T(8,128)S(1)}, f32[512,512]{0,1:T(8,128)}, u32[]{:S(2)}, u32[]{:S(2)}) collective-permute-start(f32[512,512]{0,1:T(8,128)S(1)} %get-tuple-element.24), channel_id=1, source_target_pairs={{8,0},{16,8},{24,16},{9,1},{17,9},{25,17},{10,2},{18,10},{26,18},{... | collective-permute-start | bytes 3145736 | tf_op jit(solution)/shard_map/ppermute | solution.py:21
  313.1 6.5 %copy-start = (f32[2,1024,512]{2,1,0:T(8,128)S(1)}, f32[2,1024,512]{2,1,0:T(8,128)}, u32[]{:S(2)}) copy-start(f32[2,1024,512]{2,1,0:T(8,128)} %all-reduce.2.cloned.1.call-done) | copy-start | bytes 12582916
  315.2 11.6 %slice-start = ((s8[8388608]{0:T(1024)(128)(4,1)}), s8[4194304]{0:T(1024)(128)(4,1)S(1)}, s32[]{:S(2)}) async-start(s8[8388608]{0:T(1024)(128)(4,1)} %bitcast.28), calls=%async_computation.2 | async-start | bytes 8388608
  315.4 11.4 %slice-start.1 = ((s8[8388608]{0:T(1024)(128)(4,1)}), s8[4194304]{0:T(1024)(128)(4,1)S(1)}, s32[]{:S(2)}) async-start(s8[8388608]{0:T(1024)(128)(4,1)} %bitcast.28), calls=%async_computation.3 | async-start | bytes 8388608
  315.4 4.2 collective-permute-start.7
  334.2 2.7 collective-permute-start.8
  337.4 28.2 %collective-permute-start.10 = (f32[512,512]{0,1:T(8,128)S(1)}, f32[512,512]{0,1:T(8,128)S(1)}, u32[]{:S(2)}, u32[]{:S(2)}) collective-permute-start(f32[512,512]{0,1:T(8,128)S(1)} %get-tuple-element.9), channel_id=1, source_target_pairs={{2,0},{3,1},{4,2},{5,3},{6,4},{7,5},{10,8},{11,9},{12,10},{13,11},... | collective-permute-start | bytes 3145736 | tf_op jit(solution)/shard_map/ppermute | solution.py:21
  343.0 26.8 %collective-permute-start.9 = (f32[512,512]{0,1:T(8,128)S(1)}, f32[512,512]{0,1:T(8,128)S(1)}, u32[]{:S(2)}, u32[]{:S(2)}) collective-permute-start(f32[512,512]{0,1:T(8,128)S(1)} %get-tuple-element.8), channel_id=1, source_target_pairs={{0,2},{1,3},{2,4},{3,5},{4,6},{5,7},{8,10},{9,11},{10,12},{11,13},... | collective-permute-start | bytes 3145736 | tf_op jit(solution)/shard_map/ppermute | solution.py:21
  370.2 2.7 collective-permute-start.11
  373.5 27.1 %collective-permute-start.12 = (f32[512,512]{0,1:T(8,128)S(1)}, f32[512,512]{0,1:T(8,128)S(1)}, u32[]{:S(2)}, u32[]{:S(2)}) collective-permute-start(f32[512,512]{0,1:T(8,128)S(1)} %get-tuple-element.19), channel_id=1, source_target_pairs={{0,8},{8,16},{16,24},{1,9},{9,17},{17,25},{2,10},{10,18},{18,26},{... | collective-permute-start | bytes 3145736 | tf_op jit(solution)/shard_map/ppermute | solution.py:21
  375.4 45.4 %collective-permute-start.13 = (f32[512,512]{0,1:T(8,128)S(1)}, f32[512,512]{0,1:T(8,128)S(1)}, u32[]{:S(2)}, u32[]{:S(2)}) collective-permute-start(f32[512,512]{0,1:T(8,128)S(1)} %get-tuple-element.20), channel_id=1, source_target_pairs={{8,0},{16,8},{24,16},{9,1},{17,9},{25,17},{10,2},{18,10},{26,18},{... | collective-permute-start | bytes 3145736 | tf_op jit(solution)/shard_map/ppermute | solution.py:21
Sparse Core Ops, SparseCore 0:
  9.0 80.5 all-gather.2
  94.3 104.8 all-reduce.1
where the time goes:
time: 433 us; the launch traced here: 430 us
  waiting for transfers between devices  333 us (77%)
  matrix products  33.7 us (8%)
  starting transfers between devices  26.2 us (6%)
  other arithmetic  17.4 us (4%)
  between operations  13.7 us (3%)
  local copies, waits for them, and re-layouts  5.69 us (1%)
    ppermute x8, waiting for transfers between devices, passed_along(): lax.ppermute(value, axis, [(source, source + steps) for source in range(f...  133 us
    psum x1, waiting for transfers between devices, broadcast(): return lax.psum(block, axis)  98.7 us
    all_gather x1, waiting for transfers between devices, shards(): whole_all = lax.all_gather(rotations[:, 0], 'col', axis=1, tiled=True)  82.2 us
    ppermute x8, starting transfers between devices, passed_along(): lax.ppermute(value, axis, [(source, source + steps) for source in range(f...  25.5 us
    ppermute x6, waiting for transfers between devices, from_partner(): return lax.ppermute(value, axis, pairs)  19 us
    dot_general x2, matrix products, mix_rows(): lax.dot_general(turn, mixed, (((0,), (0,)), ((), ())), precision=lax.Prec...  16.4 us
    dot_general x2, matrix products, shards(): jnp.dot(second, column_turn[width:], precision=lax.Precision.HIGHEST, pre...  8.96 us
  transfers between devices with their start and end apart: 16, of which 16 were waited for; matrix products, arithmetic and copies ran while one was open for 0% of the time, Pallas kernels for 0%

commit v1 on v0

v1 whole, which is shorter than its diff:
```python
import functools

import jax
import jax.numpy as jnp
from jax import lax
from jax.experimental import pallas as pl
from jax.experimental.pallas import tpu as pltpu
from jax.sharding import PartitionSpec as P

MESH = pl.DeviceIdType.MESH
TILE = 256


def pick(cond, yes, no):
    return jnp.where(cond, jnp.int32(yes), jnp.int32(no))


def goes_to(n, pair, odd):
    even_pair = pick(pair == 0, 0, pick(pair == n - 1, n - 1, pair + 1))
    even_half = pick(pair == n - 1, 1, 0)
    odd_pair = pick(pair == 0, 1, pair - 1)
    odd_half = pick(pair == 0, 0, 1)
    return pick(odd == 0, even_pair, odd_pair), pick(odd == 0, even_half, odd_half)


def comes_from(n, pair, odd):
    even_pair = pick(pair == 0, 0, pair - 1)
    even_half = pick(pair == 1, 1, 0)
    odd_pair = pick(pair == n - 1, n - 1, pair + 1)
    odd_half = pick(pair == n - 1, 0, 1)
    return pick(odd == 0, even_pair, odd_pair), pick(odd == 0, even_half, odd_half)


def ring_next(n, r, direction):
    order = [i ^ (i >> 1) for i in range(n)]
    result = jnp.int32(0)
    for i in range(n):
        result = pick(r == order[i], order[(i + direction) % n], result)
    return result


def split(x):
    hi = x.astype(jnp.bfloat16)
    lo = (x - hi.astype(jnp.float32)).astype(jnp.bfloat16)
    return hi, lo


def dot(a, b):
    return jnp.dot(a, b, preferred_element_type=jnp.float32)


def kernel(
    n, gram, rot, out, X, V, T, C, res, Xh, Xl, Bh, Bl,
    xsend, xrecv, vsend, vrecv, tsend, trecv, msend, mrecv,
):
    r = lax.axis_index("row")
    c = lax.axis_index("col")
    z = c // 2
    p = c % 2
    steps, h, size = rot.shape
    half = size // 2
    succ = ring_next(n, r, 1)
    pred = ring_next(n, r, -1)
    partner = (r, c + 1 - 2 * p)
    up = (r, c + 2)
    down = (r, c - 2)
    is_root = r == z
    pending = []

    def remote(src, dst, send, recv, device):
        return pltpu.make_async_remote_copy(
            src_ref=src, dst_ref=dst, send_sem=send, recv_sem=recv,
            device_id=device, device_id_type=MESH,
        )

    def x_rows(s, cc):
        return X.at[s, pl.ds(pl.multiple_of(cc * h, h), h), :]

    def x_copy(s, cc, way):
        device = (up, down, partner)[way]
        rows = x_rows(s, cc)
        return remote(rows, rows, xsend.at[s, cc, way], xrecv.at[s, cc], device)

    def v_copy(s, cc, q, root):
        rows = pl.ds(pl.multiple_of(cc * h, h), h)
        dst = V.at[s, rows, :]
        src = X.at[s, rows, pl.ds(pl.multiple_of(p * half, half), half)] if root else dst
        device = ((succ if q == 0 else pred), c)
        return remote(src, dst, vsend.at[s, cc], vrecv.at[s, cc], device)

    def go(cond, make):
        def begin():
            make().start()
        def end():
            make().wait_send()
        if cond is None:
            begin()
        else:
            pl.when(cond)(begin)
        pending.append((cond, end))

    targets = []
    to_pair, to_odd = goes_to(n, z, p)
    to_col = 2 * to_pair + to_odd
    for a in range(2):
        to_row, slot = goes_to(n, r, jnp.int32(a))
        stays = jnp.logical_and(to_row == r, to_col == c)
        targets.append((to_row, slot, stays))
    origins = []
    from_pair, from_odd = comes_from(n, z, p)
    from_col = 2 * from_pair + from_odd
    for a in range(2):
        from_row, _ = comes_from(n, r, jnp.int32(a))
        stays = jnp.logical_and(from_row == r, from_col == c)
        origins.append((from_row, stays))

    barrier = pltpu.get_barrier_semaphore()

    def hello(device):
        pl.semaphore_signal(barrier, inc=1, device_id=device, device_id_type=MESH)

    count = jnp.int32(3)
    hello(partner)
    hello((succ, c))
    hello((pred, c))
    pl.when(z < n - 1)(lambda: hello(up))
    pl.when(z > 0)(lambda: hello(down))
    count = count + pick(z < n - 1, 1, 0) + pick(z > 0, 1, 0)
    for a in range(2):
        to_row, _, stays = targets[a]
        pl.when(jnp.logical_not(stays))(lambda to_row=to_row: hello((to_row, to_col)))
        count = count + pick(stays, 0, 1)
        from_row, stays = origins[a]
        pl.when(jnp.logical_not(stays))(lambda from_row=from_row: hello((from_row, from_col)))
        count = count + pick(stays, 0, 1)
    pl.semaphore_wait(barrier, count)

    def roots(s, zs, cond):
        for q in range(2):
            here = is_root if cond is None else jnp.logical_and(is_root, cond)
            go(here, lambda q=q: v_copy(s, 2 * zs + q, q, True))

    def start_own(s):
        X[s, pl.ds(pl.multiple_of(c * h, h), h), :] = rot[s]
        go(z < n - 1, lambda: x_copy(s, c, 0))
        go(z > 0, lambda: x_copy(s, c, 1))
        go(None, lambda: x_copy(s, c, 2))

    def finish_own(s):
        x_copy(s, 2 * z + 1 - p, 2).wait_recv()
        roots(s, z, None)

    def sides(d):
        return ((0, z - d, z >= d), (1, z + d, z + d < n))

    def service(s, d):
        for way, zs, exists in sides(d):
            cc = 2 * zs + p
            pl.when(exists)(lambda cc=cc, way=way: x_copy(s, cc, way).wait_recv())
            if d < n - 1:
                onward = z < n - 1 if way == 0 else z > 0
                go(jnp.logical_and(exists, onward), lambda cc=cc, way=way: x_copy(s, cc, way))
            go(exists, lambda cc=cc: x_copy(s, cc, 2))
        for way, zs, exists in sides(d):
            cc = 2 * zs + 1 - p
            pl.when(exists)(lambda cc=cc: x_copy(s, cc, 2).wait_recv())
            roots(s, zs, exists)

    def relay(s, d):
        group = ((0, z, None),) if d == 0 else sides(d)
        for _, zs, exists in group:
            for q in range(2):
                cc = 2 * zs + q
                here = jnp.logical_not(is_root)
                if exists is not None:
                    here = jnp.logical_and(here, exists)
                pl.when(here)(lambda cc=cc, q=q: v_copy(s, cc, q, False).wait_recv())
                further = (succ if q == 0 else pred) != z
                go(jnp.logical_and(here, further), lambda cc=cc, q=q: v_copy(s, cc, q, False))

    def split_x(s):
        @pl.loop(0, size // TILE)
        def _(i):
            rows = pl.ds(pl.multiple_of(i * TILE, TILE), TILE)
            hi, lo = split(X[s, rows, :].T)
            Xh[:, rows] = hi
            Xl[:, rows] = lo

    def split_b(load):
        @pl.loop(0, size // TILE)
        def _(i):
            rows = pl.ds(pl.multiple_of(i * TILE, TILE), TILE)
            hi, lo = split(load(rows))
            Bh[rows, :] = hi
            Bl[rows, :] = lo

    def split_v(s):
        columns = pl.ds(pl.multiple_of(p * half, half), half)
        pl.when(is_root)(lambda: split_b(lambda rows: X[s, rows, columns]))
        pl.when(jnp.logical_not(is_root))(lambda: split_b(lambda rows: V[s, rows, :]))

    def t_copy(s, a):
        part = T.at[s, p, pl.ds(a * half, half), :]
        return remote(part, part, tsend.at[s, a], trecv.at[s, a], partner)

    def turn(s):
        for a in range(2):
            @pl.loop(0, half // TILE)
            def _(i):
                rows = pl.ds(pl.multiple_of(a * half + i * TILE, TILE), TILE)
                hi = Xh[rows, :]
                T[s, p, rows, :] = dot(hi, Bh[...]) + dot(hi, Bl[...]) + dot(Xl[rows, :], Bh[...])
            go(None, lambda a=a: t_copy(s, a))

    def m_copy(s, a):
        to_row, slot, _ = targets[a]
        landing = C if s < steps - 1 else out
        dst = landing.at[pl.ds(pl.multiple_of(slot * half, half), half), :] if s == steps - 1 \
            else landing.at[s, pl.ds(pl.multiple_of(slot * half, half), half), :]
        src = res.at[s, pl.ds(a * half, half), :]
        return src, dst, slot, to_row

    def m_remote(s, a):
        src, dst, slot, to_row = m_copy(s, a)
        return remote(src, dst, msend.at[s, a], mrecv.at[s, slot], (to_row, to_col))

    def m_local(s, a):
        src, dst, slot, _ = m_copy(s, a)
        return pltpu.make_async_copy(src, dst, mrecv.at[s, slot])

    def mix(s):
        for a in range(2):
            t_copy(s, a).wait_recv()

            @pl.loop(0, half // TILE)
            def _(i):
                rows = pl.ds(pl.multiple_of(a * half + i * TILE, TILE), TILE)
                total = jnp.zeros((TILE, half), jnp.float32)
                for q in range(2):
                    hi, lo = split(T[s, q, rows, :])
                    bh = Bh[q * half:(q + 1) * half, :]
                    bl = Bl[q * half:(q + 1) * half, :]
                    total = total + (dot(hi, bh) + dot(hi, bl) + dot(lo, bh))
                res[s, rows, :] = total
            stays = targets[a][2]
            pl.when(stays)(lambda a=a: m_local(s, a).start())
            go(jnp.logical_not(stays), lambda a=a: m_remote(s, a))

    def arrive(s):
        for a in range(2):
            src = res.at[s, pl.ds(0, half), :]
            dst = (C.at[s] if s < steps - 1 else out).at[pl.ds(a * half, half), :]
            pltpu.make_async_copy(src, dst, mrecv.at[s, a]).wait()

    start_own(0)
    finish_own(0)
    for d in range(1, n):
        service(0, d)
        if d == n - 2 or n == 2:
            start_own(1)
        if d >= 2:
            relay(0, d - 2)
    split_x(0)
    split_b(lambda rows: gram[rows, :])
    turn(0)
    for d in range(max(n - 2, 0), n - 1):
        relay(0, d)
    finish_own(1)
    service(1, 1)
    relay(0, n - 1)
    split_v(0)
    mix(0)
    for d in range(2, n):
        service(1, d)
        relay(1, d - 2)
    split_x(1)
    for d in range(max(n - 2, 0), n):
        relay(1, d)
    arrive(0)
    split_b(lambda rows: C[0, rows, :])
    turn(1)
    split_v(1)
    mix(1)
    arrive(1)
    for cond, end in pending:
        if cond is None:
            end()
        else:
            pl.when(cond)(end)


def shards(gram, rotations):
    n = lax.axis_size("row")
    n_col = lax.axis_size("col")
    steps, _, h, size = rotations.shape
    half = size // 2
    f32, bf16 = jnp.float32, jnp.bfloat16
    dma = pltpu.SemaphoreType.DMA
    vmem = pl.BlockSpec(memory_space=pltpu.VMEM)
    flops = steps * 2 * 2 * size * size * half * 3
    return pl.pallas_call(
        functools.partial(kernel, n),
        out_shape=jax.ShapeDtypeStruct(gram.shape, f32),
        in_specs=[vmem, vmem],
        out_specs=vmem,
        scratch_shapes=[
            pltpu.VMEM((steps, size, size), f32),
            pltpu.VMEM((steps, size, half), f32),
            pltpu.VMEM((steps, 2, size, half), f32),
            pltpu.VMEM((steps - 1, size, half), f32),
            pltpu.VMEM((steps, size, half), f32),
            pltpu.VMEM((size, size), bf16),
            pltpu.VMEM((size, size), bf16),
            pltpu.VMEM((size, half), bf16),
            pltpu.VMEM((size, half), bf16),
            dma((steps, n_col, 3)),
            dma((steps, n_col)),
            dma((steps, n_col)),
            dma((steps, n_col)),
            dma((steps, 2)),
            dma((steps, 2)),
            dma((steps, 2)),
            dma((steps, 2)),
        ],
        compiler_params=pltpu.CompilerParams(
            collective_id=0, has_side_effects=True, vmem_limit_bytes=56 * 1024 * 1024
        ),
        cost_estimate=pl.CostEstimate(flops=flops, bytes_accessed=8 * 1024 * 1024, transcendentals=0),
    )(gram, rotations.reshape(steps, h, size))


def solution(mesh):
    placed = (P("row", "col"), P(None, "row", "col", None))
    return jax.shard_map(
        shards, mesh=mesh, in_specs=placed, out_specs=P("row", "col"), check_vma=False
    )
```

time: 433 us -> 389 us (0.90)
  Pallas kernels: 0 us -> 385 us
  waiting for transfers between devices: 333 us -> 0 us
  matrix products: 33.7 us -> 0 us
  starting transfers between devices: 26.2 us -> 0 us
  other arithmetic: 17.4 us -> 0 us
  between operations: 13.7 us -> 0.01 us
    pallas_call x0 -> x1, Pallas kernels: none -> 385 us  [shards(): pl.pallas_call(functools.partial(kernel, n), out_shape=jax.ShapeDtypeStru...]
    ppermute x14 -> x0, waiting for transfers between devices: 152 us -> none  [the longest x8 133 us: passed_along(): lax.ppermute(value, axis, [(source, source + steps) for source in range(f...]
    psum x1 -> x0, waiting for transfers between devices: 98.7 us -> none  [broadcast(): return lax.psum(block, axis)]
    all_gather x1 -> x0, waiting for transfers between devices: 82.2 us -> none  [shards(): whole_all = lax.all_gather(rotations[:, 0], 'col', axis=1, tiled=True)]
    dot_general x6 -> x0, matrix products: 33.7 us -> none  [the longest x2 16.4 us: mix_rows(): lax.dot_general(turn, mixed, (((0,), (0,)), ((), ())), precision=lax.Prec...]
    ppermute x14 -> x0, starting transfers between devices: 26.2 us -> none  [the longest x8 25.5 us: passed_along(): lax.ppermute(value, axis, [(source, source + steps) for source in range(f...]
    select_n x13 -> x0, other arithmetic: 17.1 us -> none  [the longest x1 4.62 us: broadcast(): jnp.where(lax.axis_index(axis) == source, block, jnp.zeros_like(block))]
  transfers between devices with their start and end apart: 16 -> 0, of which waited for: 16 -> 0; matrix products, arithmetic and copies ran while one was open for 0% -> 0% of each run, Pallas kernels for 0% -> 0%
where the time goes in v1:
time: 389 us; the launch traced here: 388 us
  Pallas kernels  385 us (99%)
    pallas_call x1, Pallas kernels, shards(): pl.pallas_call(functools.partial(kernel, n), out_shape=jax.ShapeDtypeStru...  385 us

profile of v1, /device:TPU:26, one launch (start us, length us, event | category | flops | bytes accessed | tf_op | source)
XLA Modules:
  0.0 388.0 jit_solution(6382360711918795360)
XLA Ops:
  0.0 384.9 %shard_map.28 = f32[1024,512]{1,0:T(8,128)} custom-call(f32[1024,512]{1,0:T(8,128)} %gram.1, f32[2,128,1024]{2,1,0:T(8,128)} %bitcast.1), custom_call_target="tpu_custom_call" | custom-call | flops 12884901888 | bytes 8388608 | tf_op jit(solution)/shard_map/pallas_call | solution.py:301
  384.9 3.1 copy.4

commit v2 on v1

--- a/solution.py
+++ b/solution.py
@@ -135,10 +135,15 @@
         count = count + pick(stays, 0, 1)
     pl.semaphore_wait(barrier, count)
 
+    def keep_half(s, cc):
+        rows = pl.ds(pl.multiple_of(cc * h, h), h)
+        V[s, rows, :] = X[s, rows, pl.ds(pl.multiple_of(p * half, half), half)]
+
     def roots(s, zs, cond):
         for q in range(2):
             here = is_root if cond is None else jnp.logical_and(is_root, cond)
-            go(here, lambda q=q: v_copy(s, 2 * zs + q, q, True))
+            pl.when(here)(lambda q=q: keep_half(s, 2 * zs + q))
+            go(here, lambda q=q: v_copy(s, 2 * zs + q, q, False))
 
     def start_own(s):
         X[s, pl.ds(pl.multiple_of(c * h, h), h), :] = rot[s]

time: 389 us -> 389 us (level)
  no operation moved by 1% of the time
where the time goes in v2:
time: 389 us; the launch traced here: 388 us
  Pallas kernels  385 us (99%)
    pallas_call x1, Pallas kernels, shards(): pl.pallas_call(functools.partial(kernel, n), out_shape=jax.ShapeDtypeStru...  385 us

profile of v2, /device:TPU:26, one launch (start us, length us, event | category | flops | bytes accessed | tf_op | source)
XLA Modules:
  0.0 388.0 jit_solution(4097029607704113206)
XLA Ops:
  0.0 384.9 %shard_map.28 = f32[1024,512]{1,0:T(8,128)} custom-call(f32[1024,512]{1,0:T(8,128)} %gram.1, f32[2,128,1024]{2,1,0:T(8,128)} %bitcast.1), custom_call_target="tpu_custom_call" | custom-call | flops 12884901888 | bytes 8388608 | tf_op jit(solution)/shard_map/pallas_call | solution.py:306
  384.9 3.1 copy.4

commit v3 on v1

--- a/solution.py
+++ b/solution.py
@@ -166,17 +166,26 @@
             pl.when(exists)(lambda cc=cc: x_copy(s, cc, 2).wait_recv())
             roots(s, zs, exists)
 
-    def relay(s, d):
+    def v_shards(d):
         group = ((0, z, None),) if d == 0 else sides(d)
         for _, zs, exists in group:
             for q in range(2):
-                cc = 2 * zs + q
                 here = jnp.logical_not(is_root)
                 if exists is not None:
                     here = jnp.logical_and(here, exists)
-                pl.when(here)(lambda cc=cc, q=q: v_copy(s, cc, q, False).wait_recv())
-                further = (succ if q == 0 else pred) != z
-                go(jnp.logical_and(here, further), lambda cc=cc, q=q: v_copy(s, cc, q, False))
+                yield 2 * zs + q, q, here, (succ if q == 0 else pred) != z
+
+    def relay(s, d):
+        for cc, q, here, further in v_shards(d):
+            onward = jnp.logical_and(here, further)
+            pl.when(onward)(lambda cc=cc, q=q: v_copy(s, cc, q, False).wait_recv())
+            go(onward, lambda cc=cc, q=q: v_copy(s, cc, q, False))
+
+    def finish_v(s):
+        for d in range(n):
+            for cc, q, here, further in v_shards(d):
+                ends = jnp.logical_and(here, jnp.logical_not(further))
+                pl.when(ends)(lambda cc=cc, q=q: v_copy(s, cc, q, False).wait_recv())
 
     def split_x(s):
         @pl.loop(0, size // TILE)
@@ -258,27 +267,26 @@
         service(0, d)
         if d == n - 2 or n == 2:
             start_own(1)
-        if d >= 2:
-            relay(0, d - 2)
+        relay(0, d - 1)
     split_x(0)
     split_b(lambda rows: gram[rows, :])
+    relay(0, n - 1)
     turn(0)
-    for d in range(max(n - 2, 0), n - 1):
-        relay(0, d)
     finish_own(1)
     service(1, 1)
-    relay(0, n - 1)
+    relay(1, 0)
+    finish_v(0)
     split_v(0)
     mix(0)
     for d in range(2, n):
         service(1, d)
-        relay(1, d - 2)
+        relay(1, d - 1)
     split_x(1)
-    for d in range(max(n - 2, 0), n):
-        relay(1, d)
+    relay(1, n - 1)
     arrive(0)
     split_b(lambda rows: C[0, rows, :])
     turn(1)
+    finish_v(1)
     split_v(1)
     mix(1)
     arrive(1)

time: 389 us -> 204 us (0.52)
  the two profiles are of different devices: /device:TPU:26 before, /device:TPU:5 now
where the time goes in v3:
time: 204 us
  Pallas kernels  201 us (99%)
  local copies, waits for them, and re-layouts  3.08 us (2%)
    pallas_call x1, Pallas kernels, shards(): pl.pallas_call(functools.partial(kernel, n), out_shape=jax.ShapeDtypeStru...  201 us

profile of v3, /device:TPU:5, one launch (start us, length us, event | category | flops | bytes accessed | tf_op | source)
XLA Modules:
  0.0 203.7 jit_solution(15383110090114817480)
XLA Ops:
  0.0 200.6 %shard_map.28 = f32[1024,512]{1,0:T(8,128)} custom-call(f32[1024,512]{1,0:T(8,128)} %gram.1, f32[2,128,1024]{2,1,0:T(8,128)} %bitcast.1), custom_call_target="tpu_custom_call" | custom-call | flops 12884901888 | bytes 8388608 | tf_op jit(solution)/shard_map/pallas_call | solution.py:309
  200.6 3.1 %copy.4 = f32[1024,512]{1,0:T(8,128)} copy(f32[1024,512]{1,0:T(8,128)} %shard_map.28) | data formatting | bytes 4194304

commit v4 on v3

--- a/solution.py
+++ b/solution.py
@@ -221,29 +221,27 @@
                 T[s, p, rows, :] = dot(hi, Bh[...]) + dot(hi, Bl[...]) + dot(Xl[rows, :], Bh[...])
             go(None, lambda a=a: t_copy(s, a))
 
-    def m_copy(s, a):
+    def m_copy(s, a, i):
         to_row, slot, _ = targets[a]
-        landing = C if s < steps - 1 else out
-        dst = landing.at[pl.ds(pl.multiple_of(slot * half, half), half), :] if s == steps - 1 \
-            else landing.at[s, pl.ds(pl.multiple_of(slot * half, half), half), :]
-        src = res.at[s, pl.ds(a * half, half), :]
+        landing = C.at[s] if s < steps - 1 else out
+        dst = landing.at[pl.ds(pl.multiple_of(slot * half + i * TILE, TILE), TILE), :]
+        src = res.at[s, pl.ds(a * half + i * TILE, TILE), :]
         return src, dst, slot, to_row
 
-    def m_remote(s, a):
-        src, dst, slot, to_row = m_copy(s, a)
-        return remote(src, dst, msend.at[s, a], mrecv.at[s, slot], (to_row, to_col))
-
-    def m_local(s, a):
-        src, dst, slot, _ = m_copy(s, a)
-        return pltpu.make_async_copy(src, dst, mrecv.at[s, slot])
+    def m_remote(s, a, i):
+        src, dst, slot, to_row = m_copy(s, a, i)
+        return remote(src, dst, msend.at[s, a, i], mrecv.at[s, slot, i], (to_row, to_col))
+
+    def m_local(s, a, i):
+        src, dst, slot, _ = m_copy(s, a, i)
+        return pltpu.make_async_copy(src, dst, mrecv.at[s, slot, i])
 
     def mix(s):
         for a in range(2):
             t_copy(s, a).wait_recv()
-
-            @pl.loop(0, half // TILE)
-            def _(i):
-                rows = pl.ds(pl.multiple_of(a * half + i * TILE, TILE), TILE)
+            stays = targets[a][2]
+            for i in range(half // TILE):
+                rows = pl.ds(a * half + i * TILE, TILE)
                 total = jnp.zeros((TILE, half), jnp.float32)
                 for q in range(2):
                     hi, lo = split(T[s, q, rows, :])
@@ -251,15 +249,15 @@
                     bl = Bl[q * half:(q + 1) * half, :]
                     total = total + (dot(hi, bh) + dot(hi, bl) + dot(lo, bh))
                 res[s, rows, :] = total
-            stays = targets[a][2]
-            pl.when(stays)(lambda a=a: m_local(s, a).start())
-            go(jnp.logical_not(stays), lambda a=a: m_remote(s, a))
+                pl.when(stays)(lambda a=a, i=i: m_local(s, a, i).start())
+                go(jnp.logical_not(stays), lambda a=a, i=i: m_remote(s, a, i))
 
     def arrive(s):
         for a in range(2):
-            src = res.at[s, pl.ds(0, half), :]
-            dst = (C.at[s] if s < steps - 1 else out).at[pl.ds(a * half, half), :]
-            pltpu.make_async_copy(src, dst, mrecv.at[s, a]).wait()
+            for i in range(half // TILE):
+                src = res.at[s, pl.ds(0, TILE), :]
+                dst = (C.at[s] if s < steps - 1 else out).at[pl.ds(a * half + i * TILE, TILE), :]
+                pltpu.make_async_copy(src, dst, mrecv.at[s, a, i]).wait()
 
     start_own(0)
     finish_own(0)
@@ -327,8 +325,8 @@
             dma((steps, n_col)),
             dma((steps, 2)),
             dma((steps, 2)),
-            dma((steps, 2)),
-            dma((steps, 2)),
+            dma((steps, 2, half // TILE)),
+            dma((steps, 2, half // TILE)),
         ],
         compiler_params=pltpu.CompilerParams(
             collective_id=0, has_side_effects=True, vmem_limit_bytes=56 * 1024 * 1024

time: 204 us -> 203 us (level)
  no operation moved by 1% of the time
where the time goes in v4:
time: 203 us
  Pallas kernels  200 us (99%)
  local copies, waits for them, and re-layouts  3.08 us (2%)
    pallas_call x1, Pallas kernels, shards(): pl.pallas_call(functools.partial(kernel, n), out_shape=jax.ShapeDtypeStru...  200 us

profile of v4, /device:TPU:5, one launch (start us, length us, event | category | flops | bytes accessed | tf_op | source)
XLA Modules:
  0.0 202.8 jit_solution(5812123644126014277)
XLA Ops:
  0.0 199.7 %shard_map.28 = f32[1024,512]{1,0:T(8,128)} custom-call(f32[1024,512]{1,0:T(8,128)} %gram.1, f32[2,128,1024]{2,1,0:T(8,128)} %bitcast.1), custom_call_target="tpu_custom_call" | custom-call | flops 12884901888 | bytes 8388608 | tf_op jit(solution)/shard_map/pallas_call | solution.py:307
  199.7 3.1 %copy.4 = f32[1024,512]{1,0:T(8,128)} copy(f32[1024,512]{1,0:T(8,128)} %shard_map.28) | data formatting | bytes 4194304

commit v5 on v4

--- a/solution.py
+++ b/solution.py
@@ -272,10 +272,10 @@
     turn(0)
     finish_own(1)
     service(1, 1)
-    relay(1, 0)
     finish_v(0)
     split_v(0)
     mix(0)
+    relay(1, 0)
     for d in range(2, n):
         service(1, d)
         relay(1, d - 1)

time: 203 us -> 214 us (1.054)
  the two profiles are of different devices: /device:TPU:5 before, /device:TPU:26 now
where the time goes in v5:
time: 214 us
  Pallas kernels  211 us (99%)
  local copies, waits for them, and re-layouts  3.08 us (1%)
    pallas_call x1, Pallas kernels, shards(): pl.pallas_call(functools.partial(kernel, n), out_shape=jax.ShapeDtypeStru...  211 us

profile of v5, /device:TPU:26, one launch (start us, length us, event | category | flops | bytes accessed | tf_op | source)
XLA Modules:
  0.0 213.7 jit_solution(7568685502566728220)
XLA Ops:
  0.0 210.6 %shard_map.28 = f32[1024,512]{1,0:T(8,128)} custom-call(f32[1024,512]{1,0:T(8,128)} %gram.1, f32[2,128,1024]{2,1,0:T(8,128)} %bitcast.1), custom_call_target="tpu_custom_call" | custom-call | flops 12884901888 | bytes 8388608 | tf_op jit(solution)/shard_map/pallas_call | solution.py:307
  210.6 3.1 %copy.4 = f32[1024,512]{1,0:T(8,128)} copy(f32[1024,512]{1,0:T(8,128)} %shard_map.28) | data formatting | bytes 4194304
